TPU v7x, 256 devices: a whole 4x4x8 slice. The times are simulated.
256 devices in a mesh: dp: 32 (over z, y_hi, core), tensor: 8 (over x, y_lo).
Axes of the slice: x: 4, y: 4 (y_hi: 2, y_lo: 2; y = y_hi * 2 + y_lo), z: 8, core: 2. Of those that a mesh axis runs over, the one named last changes fastest.
Arguments:
- layer_input: bfloat16 [512, 8192], P('dp', 'tensor'), may hold values from -6 to 6
- out_cotangent: bfloat16 [512, 8192], P('dp', 'tensor'), may hold values from -6 to 6
- old_gate: bfloat16 [8192, 16384], P('tensor', 'dp'), may hold values from -0.0625 to 0.0625
- old_up: bfloat16 [8192, 16384], P('tensor', 'dp'), may hold values from -0.0625 to 0.0625
- old_down: bfloat16 [8192, 16384], P('tensor', 'dp'), may hold values from -0.046875 to 0.046875
Outputs:
- layer_out: bfloat16 [512, 8192], P('dp', 'tensor')
- token_grad: bfloat16 [512, 8192], P('dp', 'tensor')
- gate_weight_grad: bfloat16 [4096, 32768], P('tensor', 'dp')
- up_weight_grad: bfloat16 [4096, 32768], P('tensor', 'dp')
- down_weight_grad: bfloat16 [4096, 32768], P('tensor', 'dp')
All inputs are finite; a program needn't handle non-finite values.
Results may differ from a plain program's by a relative error of at most 0.02.
Values may be sent and summed in bfloat16 or wider, within the bound.
A program may use at most 64 MiB of HBM per device.

v0:
```python
import jax
import jax.numpy as jnp
from jax import lax
from jax.sharding import PartitionSpec as P


def partner(x, axis, distance):
    return lax.ppermute(x, axis, [(i, i ^ 1 << distance) for i in range(lax.axis_size(axis))])


def silu_parts(gate_value):
    sigma = jax.nn.sigmoid(gate_value)
    return (gate_value * sigma, sigma * (1.0 + gate_value * (1.0 - sigma)))


def token_rows(values):
    return lax.all_gather(values, "dp", axis=0, tiled=True)


def gather_units(values):
    return lax.all_gather(values, "tensor", axis=0, tiled=True)


def feature_sums(term_fn, out_rows):
    return lax.psum_scatter(
        term_fn(jnp.int32(0), out_rows * lax.axis_size("dp")).astype(jnp.bfloat16),
        "dp",
        scatter_dimension=0,
        tiled=True,
    ).astype(jnp.float32)


def pick_half(values, which):
    return lax.dynamic_index_in_dim(values, which, 0, keepdims=False)


def shards(layer_input, out_cotangent, old_gate, old_up, old_down):
    tensor_count = lax.axis_size("tensor")
    pair = lax.axis_index("dp") % 2
    first = pair == 0
    old_rows, old_cols = old_gate.shape
    half = old_rows // 2
    stacked = jnp.stack([old_gate, old_up, old_down], axis=0).reshape(3, 2, half, old_cols)
    stacked = jnp.swapaxes(stacked, 0, 1)
    kept = pick_half(stacked, pair)
    handed = pick_half(stacked, 1 - pair)
    taken = partner(handed, "dp", 0)
    weights = jnp.where(
        first, jnp.concatenate([kept, taken], axis=2), jnp.concatenate([taken, kept], axis=2)
    )
    gate_up = weights[:2]
    down_weight = weights[2]
    input_wide = token_rows(layer_input)
    input_all = lax.dynamic_slice_in_dim(input_wide, pair * half, half, 1)
    total_rows = input_all.shape[0]
    share_rows = total_rows // tensor_count
    own_rows = layer_input.shape[0]

    def reduce_units(term_fn):
        scattered = lax.psum_scatter(
            term_fn(jnp.int32(0), lax.axis_size("tensor") * share_rows),
            "tensor",
            scatter_dimension=0,
            tiled=True,
        )
        halves = scattered.reshape((2, share_rows // 2) + scattered.shape[1:])
        mine = pick_half(halves, pair)
        given = partner(pick_half(halves, 1 - pair), "dp", 0)
        return mine + given

    def spread_units(values):
        other = partner(values, "dp", 0)
        both = jnp.where(
            first,
            jnp.concatenate([values, other], axis=0),
            jnp.concatenate([other, values], axis=0),
        )
        return gather_units(both)

    def place_half(term):
        blank = jnp.zeros_like(term)
        return jnp.where(
            first, jnp.concatenate([term, blank], axis=1), jnp.concatenate([blank, term], axis=1)
        )

    def gate_term(first_row, row_count):
        return jnp.einsum("td,gdf->tgf", input_all, gate_up, preferred_element_type=jnp.float32)

    gate_up_sums = reduce_units(gate_term)
    gate_value = gate_up_sums[:, 0]
    up_value = gate_up_sums[:, 1]
    silu_value, silu_slope = silu_parts(gate_value)
    hidden = (silu_value * up_value).astype(jnp.bfloat16)
    hidden_all = spread_units(hidden)

    def output_term(first_row, row_count):
        term = lax.dot_general(
            hidden_all, down_weight, (((1,), (1,)), ((), ())), preferred_element_type=jnp.float32
        )
        return place_half(term)

    layer_out = feature_sums(output_term, own_rows).astype(jnp.bfloat16)
    cotangent_wide = token_rows(out_cotangent)
    cotangent_all = lax.dynamic_slice_in_dim(cotangent_wide, pair * half, half, 1)

    def hidden_term(first_row, row_count):
        return jnp.dot(cotangent_all, down_weight, preferred_element_type=jnp.float32)

    hidden_grad = reduce_units(hidden_term)
    gate_grad = (hidden_grad * up_value * silu_slope).astype(jnp.bfloat16)
    up_grad = (hidden_grad * silu_value).astype(jnp.bfloat16)
    pair_all = spread_units(jnp.stack([gate_grad, up_grad], axis=1))
    down_weight_grad = lax.dot_general(
        cotangent_all, hidden_all, (((0,), (0,)), ((), ())), preferred_element_type=jnp.float32
    ).astype(jnp.bfloat16)
    weight_pair_grad = jnp.einsum(
        "td,tgf->gdf", input_all, pair_all, preferred_element_type=jnp.float32
    ).astype(jnp.bfloat16)

    def input_term(first_row, row_count):
        term = jnp.einsum("tgf,gdf->td", pair_all, gate_up, preferred_element_type=jnp.float32)
        return place_half(term)

    token_grad = feature_sums(input_term, own_rows).astype(jnp.bfloat16)
    return (layer_out, token_grad, weight_pair_grad[0], weight_pair_grad[1], down_weight_grad)


def solution(mesh):
    placed = (
        P("dp", "tensor"),
        P("dp", "tensor"),
        P("tensor", "dp"),
        P("tensor", "dp"),
        P("tensor", "dp"),
    )
    return jax.shard_map(
        shards,
        mesh=mesh,
        in_specs=placed,
        out_specs=(
            P("dp", "tensor"),
            P("dp", "tensor"),
            P("tensor", "dp"),
            P("tensor", "dp"),
            P("tensor", "dp"),
        ),
        check_vma=False,
    )
```

profile of v0, /device:TPU:1, one launch (start us, length us, event | category | flops | bytes accessed | tf_op | source)
XLA Modules:
  0.0 662.3 jit_solution(11746494170745263345)
XLA Ops:
  7.2 0.0 all-gather.5.cloned.1.call-start
  7.2 0.7 all-gather.5.cloned.1.call-update
  7.9 0.0 all-gather.9.cloned.1.call-start
  8.0 2.2 pad_maximum_fusion
  10.2 1.5 dynamic-slice_bitcast_fusion.1
  11.6 3.2 collective-permute-start
  14.9 0.0 all-gather.9.cloned.1.call-update
  14.9 0.0 reduce-scatter.5.cloned.1.call-start
  15.0 3.0 collective-permute-done
  17.9 0.0 copy-start
  17.9 1.1 copy-done
  19.1 3.4 maximum_select_fusion
  22.5 70.1 %all-gather.5.cloned.1.call-done = bf16[512,1024]{1,0:T(8,128)(2,1)} async-done(((bf16[16,1024]{1,0:T(8,128)(2,1)}), bf16[512,1024]{1,0:T(8,128)(2,1)}) %all-gather.5.cloned.1.call-update) | async-done | bytes 1048592 | tf_op jit(solution)/shard_map/all_gather | solution.py:17
  92.6 4.2 fusion.2
  96.8 0.0 reduce-scatter.5.cloned.1.call-update
  96.8 0.0 reduce-scatter.9.cloned.1.call-start
  96.9 72.9 %all-gather.9.cloned.1.call-done = bf16[512,1024]{1,0:T(8,128)(2,1)} async-done(((bf16[16,1024]{1,0:T(8,128)(2,1)}), bf16[512,1024]{1,0:T(8,128)(2,1)}) %all-gather.9.cloned.1.call-update) | async-done | bytes 1048592 | tf_op jit(solution)/shard_map/all_gather | solution.py:17
  169.8 3.1 fusion.7
  172.9 0.0 reduce-scatter.9.cloned.1.call-update
  172.9 0.0 all-gather.7.cloned.1.call-start
  172.9 88.7 %reduce-scatter.5.cloned.1.call-done = f32[64,2,1024]{2,0,1:T(8,128)} async-done(((f32[512,2,1024]{2,0,1:T(8,128)}), f32[64,2,1024]{2,0,1:T(8,128)}) %reduce-scatter.5.cloned.1.call-update) | async-done | bytes 524304 | tf_op jit(solution)/shard_map/reduce_scatter | solution.py:60
  261.6 1.0 dynamic-slice_bitcast_fusion.2
  262.6 0.7 collective-permute-start.1
  263.3 54.5 %reduce-scatter.9.cloned.1.call-done = f32[64,1024]{1,0:T(8,128)} async-done(((f32[512,1024]{1,0:T(8,128)}), f32[64,1024]{1,0:T(8,128)}) %reduce-scatter.9.cloned.1.call-update) | async-done | bytes 262160 | tf_op jit(solution)/shard_map/reduce_scatter | solution.py:60
  317.8 0.9 dynamic-slice_bitcast_fusion.3
  318.8 1.6 collective-permute-start.3
  320.4 0.0 collective-permute-done.1
  320.4 1.1 bitcast_add_fusion
  321.5 0.0 collective-permute-done.3
  321.5 1.0 fusion.17
  322.5 0.4 collective-permute-start.2
  322.8 1.0 collective-permute-done.2
  323.8 0.7 maximum_select_fusion.2
  324.5 0.0 all-gather.7.cloned.1.call-update
  324.5 0.0 all-gather.11.cloned.1.call-start
  324.6 0.4 collective-permute-start.4
  324.9 1.1 collective-permute-done.4
  326.0 0.8 maximum_select_fusion.1
  326.8 0.0 all-gather.11.cloned.1.call-update
  326.8 0.0 reduce-scatter.7.cloned.1.call-start
  326.9 35.4 %all-gather.7.cloned.1.call-done = bf16[512,1024]{1,0:T(8,128)(2,1)} async-done(((bf16[64,1024]{1,0:T(8,128)(2,1)}), bf16[512,1024]{1,0:T(8,128)(2,1)}) %all-gather.7.cloned.1.call-update) | async-done | bytes 1048592 | tf_op jit(solution)/shard_map/all_gather | solution.py:21
  362.3 2.0 fusion.8
  364.2 1.2 select_convert_fusion.1
  365.4 0.0 reduce-scatter.7.cloned.1.call-update
  365.5 0.0 reduce-scatter.11.cloned.1.call-start
  365.5 55.9 %all-gather.11.cloned.1.call-done = bf16[512,2,1024]{2,0,1:T(8,128)(2,1)} async-done(((bf16[64,2,1024]{2,0,1:T(8,128)(2,1)}), bf16[512,2,1024]{2,0,1:T(8,128)(2,1)}) %all-gather.11.cloned.1.call-update) | async-done | bytes 2097168 | tf_op jit(solution)/shard_map/all_gather | solution.py:21
  421.4 2.9 fusion.4
  424.3 0.0 copy-start.1
  424.3 0.0 copy-start.2
  424.3 1.2 select_convert_fusion
  425.5 0.0 reduce-scatter.11.cloned.1.call-update
  425.5 3.2 convolution_convert_fusion
  428.7 0.0 copy-done.1
  428.7 0.0 copy-done.2
  428.7 1.3 convert_bitcast_fusion
  430.0 0.1 slice_bitcast_fusion
  430.1 1.3 copy.13
  431.5 1.3 copy.14
  432.8 104.5 %reduce-scatter.7.cloned.1.call-done = bf16[16,1024]{1,0:T(8,128)(2,1)} async-done(((bf16[512,1024]{1,0:T(8,128)(2,1)}), bf16[16,1024]{1,0:T(8,128)(2,1)}) %reduce-scatter.7.cloned.1.call-update) | async-done | bytes 32784 | tf_op jit(solution)/shard_map/reduce_scatter | solution.py:25
  537.2 118.2 %reduce-scatter.11.cloned.1.call-done = bf16[16,1024]{1,0:T(8,128)(2,1)} async-done(((bf16[512,1024]{1,0:T(8,128)(2,1)}), bf16[16,1024]{1,0:T(8,128)(2,1)}) %reduce-scatter.11.cloned.1.call-update) | async-done | bytes 32784 | tf_op jit(solution)/shard_map/reduce_scatter | solution.py:25
  (1 shorter events, 0.0 us)
Async XLA Ops:
  7.2 85.4 %all-gather.5.cloned.1.call-start = ((), (), s32[]{:S(2)}) async-start(), calls=%async_computation.4 | async-start | bytes 1081344 | tf_op jit(solution)/shard_map/all_gather | solution.py:17
  7.9 161.9 %all-gather.9.cloned.1.call-start = ((), (), s32[]{:S(2)}) async-start(), calls=%async_computation.8 | async-start | bytes 1081344 | tf_op jit(solution)/shard_map/all_gather | solution.py:17
  11.6 6.3 collective-permute-start
  14.9 246.7 %reduce-scatter.5.cloned.1.call-start = ((), (), s32[]{:S(2)}) async-start(), calls=%async_computation.5 | async-start | bytes 4718592 | tf_op jit(solution)/shard_map/reduce_scatter | solution.py:60
  17.9 1.1 copy-start
  96.8 221.0 %reduce-scatter.9.cloned.1.call-start = ((), (), s32[]{:S(2)}) async-start(), calls=%async_computation.9 | async-start | bytes 2359296 | tf_op jit(solution)/shard_map/reduce_scatter | solution.py:60
  172.9 189.4 %all-gather.7.cloned.1.call-start = ((), (), s32[]{:S(2)}) async-start(), calls=%async_computation.6 | async-start | bytes 1179648 | tf_op jit(solution)/shard_map/all_gather | solution.py:21
  262.6 57.8 %collective-permute-start.1 = (f32[32,2,1024]{2,0,1:T(8,128)S(1)}, f32[32,2,1024]{2,0,1:T(8,128)}, u32[]{:S(2)}, u32[]{:S(2)}) collective-permute-start(f32[32,2,1024]{2,0,1:T(8,128)S(1)} %dynamic-slice_bitcast_fusion.2), channel_id=1, source_target_pairs={{0,8},{8,0},{16,24},{24,16},{32,40},{40,32},{48,56},{56,48},{64,72... | collective-permute-start | bytes 786440 | tf_op jit(solution)/shard_map/ppermute | solution.py:8
  318.8 2.7 collective-permute-start.3
  322.5 1.3 collective-permute-start.2
  324.5 96.9 %all-gather.11.cloned.1.call-start = ((), (), s32[]{:S(2)}) async-start(), calls=%async_computation.10 | async-start | bytes 2359296 | tf_op jit(solution)/shard_map/all_gather | solution.py:21
  324.6 1.4 collective-permute-start.4
  326.8 210.4 %reduce-scatter.7.cloned.1.call-start = ((), (), s32[]{:S(2)}) async-start(), calls=%async_computation.7 | async-start | bytes 1081344 | tf_op jit(solution)/shard_map/reduce_scatter | solution.py:25
  365.5 290.0 %reduce-scatter.11.cloned.1.call-start = ((), (), s32[]{:S(2)}) async-start(), calls=%async_computation.11 | async-start | bytes 1081344 | tf_op jit(solution)/shard_map/reduce_scatter | solution.py:25
  424.3 4.4 copy-start.1
  424.3 4.4 copy-start.2
Sparse Core Ops, SparseCore 0:
  10.8 81.7 all-gather.4
  95.4 74.3 all-gather.8
  172.3 89.2 reduce-scatter.4
  264.0 53.7 reduce-scatter.8
  324.6 37.5 all-gather.6
  364.5 56.8 all-gather.10
  426.1 111.1 reduce-scatter.6
  542.4 112.9 reduce-scatter.10
where the time goes:
time: 667 us; the launch traced here: 662 us
  waiting for transfers between devices  606 us (91%)
  matrix products  16.6 us (2%)
  between operations  14.3 us (2%)
  other arithmetic  11.5 us (2%)
  local copies, waits for them, and re-layouts  7.25 us (1%)
    reduce_scatter x2, waiting for transfers between devices, feature_sums(): lax.psum_scatter(term_fn(jnp.int32(0), out_rows * lax.axis_size('dp')).as...  223 us
    reduce_scatter x2, waiting for transfers between devices, reduce_units(): lax.psum_scatter(term_fn(jnp.int32(0), lax.axis_size('tensor') * share_ro...  143 us
    all_gather x2, waiting for transfers between devices, token_rows(): return lax.all_gather(values, 'dp', axis=0, tiled=True)  143 us
    all_gather x2, waiting for transfers between devices, gather_units(): return lax.all_gather(values, 'tensor', axis=0, tiled=True)  91.3 us
  transfers between devices with their start and end apart: 13, of which 11 were waited for; matrix products, arithmetic and copies ran while one was open for 5% of the time, Pallas kernels for 0%

commit v1 on v0

v1 whole, which is shorter than its diff:
```python
import functools
import itertools

import jax
import jax.numpy as jnp
from jax import lax
from jax.experimental import pallas as pl
from jax.experimental.pallas import tpu as pltpu
from jax.sharding import PartitionSpec as P

MESH = pl.DeviceIdType.MESH
F32 = jnp.float32
BF16 = jnp.bfloat16

ORDER = (0, 1, -1, 2, -2, 3, -3, 4)
CHUNKS = 4
COPIES = 288


def dot(a, b):
    return jnp.dot(a, b, preferred_element_type=F32)


def dot_cols(a, b):
    return lax.dot_general(a, b, (((1,), (1,)), ((), ())), preferred_element_type=F32)


def dot_rows(a, b):
    return lax.dot_general(a, b, (((0,), (0,)), ((), ())), preferred_element_type=F32)


def kernel(
    x_ref, c_ref, wg_any, wu_any, wd_any,
    lo_ref, tg_ref, gw_any, uw_any, dw_any,
    wg, wu, wd, xg, cg, part, got, hh, hs, mine, sib_out, sib_in, ring_out, ring_in, fin_out, fin, gw,
    wsem, osem, ssem, rsem,
):
    dp = lax.axis_index("dp")
    me = lax.axis_index("tensor")
    core, yh, z = dp % 2, (dp // 2) % 2, dp // 4
    x, yl = me // 2, me % 2
    tokens, width = x_ref.shape
    units = wg_any.shape[1]
    chunk = 8 * tokens

    def at(dz, flip_y=0, flip_core=0):
        return (((z + dz + 8) % 8) * 4 + ((yh + flip_y) % 2) * 2 + (core + flip_core) % 2, me)

    def tensor_index(j):
        jx = (x, x + 1 - 2 * (x % 2), (x + 2) % 4, 3 - x)[j // 2]
        return jx * 2 + (yl + j % 2) % 2

    sibling = at(0, 0, 1)
    loads = [
        pltpu.make_async_copy(src, dst, wsem.at[i])
        for i, (src, dst) in enumerate(((wg_any, wg), (wu_any, wu), (wd_any, wd)))
    ]
    for load in loads:
        load.start()

    barrier = pltpu.get_barrier_semaphore()
    peers = [at(1), at(-1), at(1, 1), at(-1, 1), at(0, 1), sibling]
    peers += [(dp, tensor_index(j)) for j in range(1, 8)]
    for peer in peers:
        pl.semaphore_signal(barrier, inc=1, device_id=peer, device_id_type=MESH)
    pl.semaphore_wait(barrier, len(peers))

    numbers = itertools.count()
    sent = []

    def send(src, dst, device):
        number = next(numbers)
        copy = pltpu.make_async_remote_copy(
            src_ref=src, dst_ref=dst, send_sem=ssem.at[number], recv_sem=rsem.at[number],
            device_id=device, device_id_type=MESH,
        )
        copy.start()
        sent.append(copy)
        return copy

    held = (xg, cg)
    own = (x_ref, c_ref)
    due = {}

    def block(a, d, s):
        return held[a].at[pl.ds((ORDER.index(d) * 4 + s) * tokens, tokens), :]

    def share(a, d, s):
        due[a, d, s + 1] = send(block(a, d, s), block(a, d, s + 1), sibling)

    for a in (0, 1):
        due[a, -1, 0] = send(own[a], block(a, -1, 0), at(1))
        due[a, 1, 0] = send(own[a], block(a, 1, 0), at(-1))
        due[a, -1, 2] = send(own[a], block(a, -1, 2), at(1, 1))
        due[a, 1, 2] = send(own[a], block(a, 1, 2), at(-1, 1))
        due[a, 0, 2] = send(own[a], block(a, 0, 2), at(0, 1))
        due[a, 0, 1] = send(own[a], block(a, 0, 1), sibling)
    for a in (0, 1):
        held[a][0:tokens, :] = own[a][...]

    def pass_on(a, d, s):
        if d == 4:
            due[a, 4, s].wait_recv()
            share(a, 4, s)
            return
        due[a, -d, s].wait_recv()
        if d < 3 or s == 0:
            far = -(d + 1) if d < 3 else 4
            due[a, far, s] = send(block(a, -d, s), block(a, far, s), at(1))
        share(a, -d, s)
        due[a, d, s].wait_recv()
        if d < 3 or s == 2:
            due[a, d + 1, s] = send(block(a, d, s), block(a, d + 1, s), at(-1))
        share(a, d, s)

    summed = {}

    def partial_sums(k):
        rows = pl.ds(k * chunk, chunk)
        for a in (0, 1):
            for d in ORDER[2 * k : 2 * k + 2]:
                for s in (1, 3):
                    due[a, d, s].wait_recv()
        for i, (values, weight) in enumerate(((xg, wg), (xg, wu), (cg, wd))):
            if k == 0:
                loads[i].wait()
            sums = dot(values[rows, :], weight[...]).astype(BF16)
            part[k, :, :, i * units : (i + 1) * units] = sums.reshape(8, tokens, units)
        for j in (4, 5, 2, 6, 3, 7, 1):
            summed[k, j] = send(part.at[k, tensor_index(j)], got.at[k, j], (dp, tensor_index(j)))

    for d in (1, 2, 3, 4):
        for s in (0, 2):
            for a in (0, 1):
                pass_on(a, d, s)
        if d == 1:
            for a in (0, 1):
                due[a, 0, 2].wait_recv()
                share(a, 0, 2)
        partial_sums(d - 1)

    spread = {}

    def finish_units(k):
        for j in range(1, 8):
            summed[k, j].wait_recv()
        total = part[k, me].astype(F32)
        for j in range(1, 8):
            total = total + got[k, j].astype(F32)
        gate, up, grad = (total[:, i * units : (i + 1) * units] for i in range(3))
        sigma = jax.nn.sigmoid(gate)
        silu = gate * sigma
        slope = sigma * (1.0 + gate * (1.0 - sigma))
        mine_now = hh.at[k, me // 2, me % 2]
        mine_now[:, 0:units] = (silu * up).astype(BF16)
        mine_now[:, units : 2 * units] = (grad * up * slope).astype(BF16)
        mine_now[:, 2 * units :] = (grad * silu).astype(BF16)
        for j in (4, 5, 2, 6, 3, 7, 1):
            spread[k, j] = send(mine_now, mine_now, (dp, tensor_index(j)))

    handed, lent = {}, []

    def output_terms(k):
        for j in range(1, 8):
            spread[k, j].wait_recv()
        lent.append(send(hh.at[k, :, 0], hs.at[k, :, 1], sibling))
        lent.append(send(hh.at[k, :, 1], hs.at[k, :, 0], sibling))
        values = hh[k].reshape(chunk, 3 * units)
        out = dot_cols(values[:, 0:units], wd[...])
        grad = dot_cols(values[:, units : 2 * units], wg[...]) + dot_cols(values[:, 2 * units :], wu[...])
        for i, term in enumerate((out, grad)):
            term = term.reshape(2, 2, 2, tokens, width)
            mine[k, :, :, :, i * width : (i + 1) * width] = term[:, :, 0]
            sib_out[k, :, :, :, i * width : (i + 1) * width] = term[:, :, 1].astype(BF16)
        handed[k] = send(sib_out.at[k], sib_in.at[k], sibling)

    def reduced(d):
        slot = ORDER.index(d)
        return mine[slot // 2, slot % 2] + sib_in[slot // 2, slot % 2].astype(F32)

    rung = {}

    def step(d, way):
        slot = ORDER.index(d)
        value = reduced(d)
        if d == 4:
            half = 0 if way > 0 else 1
            ring_out[slot, half] = value[half].astype(BF16)
            to = ORDER.index(3 * way)
            rung[3 * way] = send(ring_out.at[slot, half], ring_in.at[to, half], at(way))
            return
        rung[d].wait_recv()
        if abs(d) == 3:
            half = 0 if way > 0 else 1
            first = value[0] + ring_in[slot, 0].astype(F32) if half == 0 else value[0]
            second = value[1] + ring_in[slot, 1].astype(F32) if half == 1 else value[1]
        else:
            first = value[0] + ring_in[slot, 0].astype(F32)
            second = value[1] + ring_in[slot, 1].astype(F32)
        ring_out[slot, 0] = first.astype(BF16)
        ring_out[slot, 1] = second.astype(BF16)
        if abs(d) == 1:
            place = 0 if way > 0 else 2
            rung["end", place] = send(ring_out.at[slot, 0], fin.at[place], at(way))
            rung["end", place + 1] = send(ring_out.at[slot, 1], fin.at[place + 1], at(way, 1))
        else:
            to = ORDER.index(d - way)
            rung[d - way] = send(ring_out.at[slot], ring_in.at[to], at(way))

    finish_units(2)
    finish_units(3)
    finish_units(1)
    finish_units(0)
    output_terms(2)
    output_terms(3)
    handed[3].wait_recv()
    step(4, 1)
    step(4, -1)
    output_terms(1)
    handed[2].wait_recv()
    step(-3, -1)
    step(3, 1)
    output_terms(0)
    handed[1].wait_recv()
    step(-2, -1)
    step(2, 1)
    handed[0].wait_recv()
    last = reduced(0)
    fin_out[...] = last[1].astype(BF16)
    rung["end", 4] = send(fin_out, fin.at[4], at(0, 1))
    step(-1, -1)
    step(1, 1)

    for copy in lent:
        copy.wait_recv()
    rows_all = CHUNKS * chunk
    half_width = width // 2
    tile = 128
    here = pl.multiple_of(core * units, units)
    there = pl.multiple_of((1 - core) * units, units)

    def weight_tile(i, carry):
        at_col = pl.multiple_of(core * half_width + i * tile, tile)
        at_row = pl.multiple_of(i * tile, tile)
        for m, values in enumerate((cg, xg, xg)):
            left = values[:, pl.ds(at_col, tile)]
            for source, place in ((hh, here), (hs, there)):
                right = source[:, :, :, :, m * units : (m + 1) * units].reshape(rows_all, units)
                gw[m, pl.ds(at_row, tile), pl.ds(place, units)] = dot_rows(left, right).astype(BF16)
        return carry

    lax.fori_loop(0, half_width // tile, weight_tile, 0)
    stores = [
        pltpu.make_async_copy(gw.at[m], dst, osem.at[m]) for m, dst in enumerate((dw_any, gw_any, uw_any))
    ]
    for store in stores:
        store.start()

    total = last[0]
    for place in range(5):
        rung["end", place].wait_recv()
        total = total + fin[place].astype(F32)
    lo_ref[...] = total[:, 0:width].astype(BF16)
    tg_ref[...] = total[:, width:].astype(BF16)
    for copy in sent:
        copy.wait_send()
    for store in stores:
        store.wait()


def shards(layer_input, out_cotangent, old_gate, old_up, old_down):
    tokens, width = layer_input.shape
    units = old_gate.shape[1]
    all_tokens = 32 * tokens
    vmem = pl.BlockSpec(memory_space=pltpu.VMEM)
    any_space = pl.BlockSpec(memory_space=pl.ANY)
    grad_shape = jax.ShapeDtypeStruct((width // 2, 2 * units), BF16)
    out_shape = jax.ShapeDtypeStruct((tokens, width), BF16)
    lo, tg, gw, uw, dw = pl.pallas_call(
        kernel,
        out_shape=(out_shape, out_shape, grad_shape, grad_shape, grad_shape),
        in_specs=[vmem, vmem, any_space, any_space, any_space],
        out_specs=[vmem, vmem, any_space, any_space, any_space],
        scratch_shapes=[
            pltpu.VMEM((width, units), BF16),
            pltpu.VMEM((width, units), BF16),
            pltpu.VMEM((width, units), BF16),
            pltpu.VMEM((all_tokens, width), BF16),
            pltpu.VMEM((all_tokens, width), BF16),
            pltpu.VMEM((CHUNKS, 8, tokens, 3 * units), BF16),
            pltpu.VMEM((CHUNKS, 8, tokens, 3 * units), BF16),
            pltpu.VMEM((CHUNKS, 4, 2, tokens, 3 * units), BF16),
            pltpu.VMEM((CHUNKS, 4, 2, tokens, 3 * units), BF16),
            pltpu.VMEM((CHUNKS, 2, 2, tokens, 2 * width), F32),
            pltpu.VMEM((CHUNKS, 2, 2, tokens, 2 * width), BF16),
            pltpu.VMEM((CHUNKS, 2, 2, tokens, 2 * width), BF16),
            pltpu.VMEM((8, 2, tokens, 2 * width), BF16),
            pltpu.VMEM((8, 2, tokens, 2 * width), BF16),
            pltpu.VMEM((tokens, 2 * width), BF16),
            pltpu.VMEM((5, tokens, 2 * width), BF16),
            pltpu.VMEM((3, width // 2, 2 * units), BF16),
            pltpu.SemaphoreType.DMA((3,)),
            pltpu.SemaphoreType.DMA((3,)),
            pltpu.SemaphoreType.DMA((COPIES,)),
            pltpu.SemaphoreType.DMA((COPIES,)),
        ],
        compiler_params=pltpu.CompilerParams(
            collective_id=0, has_side_effects=True, vmem_limit_bytes=48 * 1024 * 1024
        ),
        cost_estimate=pl.CostEstimate(
            flops=18 * all_tokens * width * units, bytes_accessed=12 * width * units, transcendentals=0
        ),
    )(layer_input, out_cotangent, old_gate, old_up, old_down)
    return lo, tg, gw, uw, dw


def solution(mesh):
    wide = P("dp", "tensor")
    stored = P("tensor", "dp")
    return jax.shard_map(
        shards,
        mesh=mesh,
        in_specs=(wide, wide, stored, stored, stored),
        out_specs=(wide, wide, stored, stored, stored),
        check_vma=False,
    )
```

time: 667 us -> 82.7 us (0.12)
  the two profiles are of different devices: /device:TPU:1 before, /device:TPU:32 now
where the time goes in v1:
time: 82.7 us; the launch traced here: 82.5 us
  Pallas kernels  73.7 us (89%)
  local copies, waits for them, and re-layouts  8.1 us (10%)
    pallas_call x1, Pallas kernels, shards(): pl.pallas_call(kernel, out_shape=(out_shape, out_shape, grad_shape, grad_...  73.7 us
    unnamed x13, local copies, waits for them, and re-layouts  8.1 us

profile of v1, /device:TPU:32, one launch (start us, length us, event | category | flops | bytes accessed | tf_op | source)
XLA Modules:
  0.0 82.5 jit_solution(18014786603023806980)
XLA Ops:
  0.6 0.0 copy-start
  0.6 1.2 %copy-done = bf16[1024,512]{1,0:T(8,128)(2,1)S(1)} copy-done((bf16[1024,512]{1,0:T(8,128)(2,1)S(1)}, bf16[1024,512]{1,0:T(8,128)(2,1)}, u32[]{:S(2)}) %copy-start) | copy-done | bytes 1048600
  1.9 0.0 copy-start.1
  1.9 1.2 %copy-done.1 = bf16[1024,512]{1,0:T(8,128)(2,1)S(1)} copy-done((bf16[1024,512]{1,0:T(8,128)(2,1)S(1)}, bf16[1024,512]{1,0:T(8,128)(2,1)}, u32[]{:S(2)}) %copy-start.1) | copy-done | bytes 1048600
  3.1 0.0 copy-start.2
  3.1 0.8 copy-done.2
  3.8 0.0 copy-start.3
  3.8 0.8 copy-done.3
  4.6 73.7 %shard_map.92 = (bf16[16,1024]{1,0:T(8,128)(2,1)S(1)}, bf16[16,1024]{1,0:T(8,128)(2,1)S(1)}, bf16[512,1024]{1,0:T(8,128)(2,1)S(1)}, bf16[512,1024]{1,0:T(8,128)(2,1)S(1)}, bf16[512,1024]{1,0:T(8,128)(2,1)S(1)}) custom-call(bf16[16,1024]{1,0:T(8,128)(2,1)S(1)} %copy-done.2, bf16[16,1024]{1,0:T(8,128)(2,1)S(1)} %copy-done.3, bf16[1024,512]{1,0:T(8,128)(2,1)S(1)} %copy-done, ...), custom_call_target="tpu_custom_call" | custom-call | flops 4831838208 | bytes 6291456 | tf_op jit(solution)/shard_map/pallas_call | solution.py:279
  78.3 0.6 copy.15
  78.9 0.6 copy.16
  79.5 1.0 %copy.17 = bf16[512,1024]{1,0:T(8,128)(2,1)} copy(bf16[512,1024]{1,0:T(8,128)(2,1)S(1)} %get-tuple-element.12) | data formatting | bytes 2097152
  80.5 1.0 %copy.18 = bf16[512,1024]{1,0:T(8,128)(2,1)} copy(bf16[512,1024]{1,0:T(8,128)(2,1)S(1)} %get-tuple-element.13) | data formatting | bytes 2097152
  81.5 1.0 %copy.19 = bf16[512,1024]{1,0:T(8,128)(2,1)} copy(bf16[512,1024]{1,0:T(8,128)(2,1)S(1)} %get-tuple-element.14) | data formatting | bytes 2097152
Async XLA Ops:
  0.6 1.2 %copy-start = (bf16[1024,512]{1,0:T(8,128)(2,1)S(1)}, bf16[1024,512]{1,0:T(8,128)(2,1)}, u32[]{:S(2)}) copy-start(bf16[1024,512]{1,0:T(8,128)(2,1)} %wg_any.1) | copy-start | bytes 3145732
  1.9 1.2 %copy-start.1 = (bf16[1024,512]{1,0:T(8,128)(2,1)S(1)}, bf16[1024,512]{1,0:T(8,128)(2,1)}, u32[]{:S(2)}) copy-start(bf16[1024,512]{1,0:T(8,128)(2,1)} %wu_any.1) | copy-start | bytes 3145732
  3.1 0.8 copy-start.2
  3.8 0.8 copy-start.3

commit v2 on v1

v2 whole, which is shorter than its diff:
```python
import jax
import jax.numpy as jnp
from jax import lax
from jax.experimental import pallas as pl
from jax.experimental.pallas import tpu as pltpu
from jax.sharding import PartitionSpec as P

MESH = pl.DeviceIdType.MESH
F32 = jnp.float32
BF16 = jnp.bfloat16

ORDER = (0, 1, -1, 2, -2, 3, -3, 4)
CHUNKS = 4
SENDS, RECEIVES = 7, 57
ENDS = ((2, 0), (2, 1), (-2, 0), (-2, 1), (1, 0), (1, 1), (-1, 0), (-1, 1), (0, 1))


def dot(a, b):
    return jnp.dot(a, b, preferred_element_type=F32)


def dot_cols(a, b):
    return lax.dot_general(a, b, (((1,), (1,)), ((), ())), preferred_element_type=F32)


def dot_rows(a, b):
    return lax.dot_general(a, b, (((0,), (0,)), ((), ())), preferred_element_type=F32)


def kernel(
    x_ref, c_ref, wg_any, wu_any, wd_any,
    lo_ref, tg_ref, gw_out,
    wg, wu, wd, xg, cg, part, got, hh, hs, mine, sib_out, sib_in, sums_out, met_in, fin, gw,
    wsem, osem, ssem, rsem,
):
    dp = lax.axis_index("dp")
    me = lax.axis_index("tensor")
    core, yh, z = dp % 2, (dp // 2) % 2, dp // 4
    x, yl = me // 2, me % 2
    tokens, width = x_ref.shape
    units = wg_any.shape[1]
    chunk = 8 * tokens

    def at(dz, flip_y=0, flip_core=0):
        return (((z + dz + 8) % 8) * 4 + ((yh + flip_y) % 2) * 2 + (core + flip_core) % 2, me)

    def tensor_index(j):
        jx = (x, x + 1 - 2 * (x % 2), (x + 2) % 4, 3 - x)[j // 2]
        return jx * 2 + (yl + j % 2) % 2

    sibling = at(0, 0, 1)
    loads = [
        pltpu.make_async_copy(src, dst, wsem.at[i])
        for i, (src, dst) in enumerate(((wg_any, wg), (wu_any, wu), (wd_any, wd)))
    ]
    mine_in = [
        pltpu.make_async_copy(src, dst.at[pl.ds(0, tokens), :], wsem.at[3 + i])
        for i, (src, dst) in enumerate(((x_ref, xg), (c_ref, cg)))
    ]
    for load in mine_in + loads:
        load.start()

    barrier = pltpu.get_barrier_semaphore()
    peers = [at(1), at(-1), at(1, 1), at(-1, 1), at(0, 1), sibling]
    peers += [at(2), at(-2), at(2, 1), at(-2, 1)]
    peers += [(dp, tensor_index(j)) for j in range(1, 8)]
    for peer in peers:
        pl.semaphore_signal(barrier, inc=1, device_id=peer, device_id_type=MESH)
    pl.semaphore_wait(barrier, len(peers))

    places = {}

    def place_of(kind, key):
        return places.setdefault((kind, key), sum(1 for k, _ in places if k == kind))

    def send(src, dst, device, key, group):
        copy = pltpu.make_async_remote_copy(
            src_ref=src, dst_ref=dst, send_sem=ssem.at[place_of("send", group)], recv_sem=rsem.at[place_of("recv", key)],
            device_id=device, device_id_type=MESH,
        )
        copy.start()

    def of_size(ref, key, group):
        return pltpu.make_async_remote_copy(
            src_ref=ref, dst_ref=ref, send_sem=ssem.at[place_of("send", group)], recv_sem=rsem.at[place_of("recv", key)],
            device_id=sibling, device_id_type=MESH,
        )

    def arrived(ref, *key):
        of_size(ref, key, "gather0").wait_recv()

    def left(ref, group):
        of_size(ref, ("gather", 0, 1, 0), group).wait_send()

    held = (xg, cg)
    own = (x_ref, c_ref)

    def block(a, d, s):
        return held[a].at[pl.ds((ORDER.index(d) * 4 + s) * tokens, tokens), :]

    def pass_to(a, src, d, s, device):
        send(src, block(a, d, s), device, ("gather", a, d, s), f"gather{a}")

    def share(a, src, d, s):
        send(src, block(a, d, s + 1), sibling, ("share", ORDER.index(d) // 2), f"gather{a}")

    def here_now(a, d, s):
        arrived(block(a, d, s), "gather", a, d, s)

    for a in (0, 1):
        pass_to(a, own[a], -1, 0, at(1))
        pass_to(a, own[a], 1, 0, at(-1))
        pass_to(a, own[a], -1, 2, at(1, 1))
        pass_to(a, own[a], 1, 2, at(-1, 1))
        pass_to(a, own[a], 0, 2, at(0, 1))
        share(a, own[a], 0, 0)

    def pass_on(a, d, s):
        for way in (1, -1):
            to = -way * d if d < 4 else 4
            if d == 4 and (way > 0) != (s == 0):
                continue
            here_now(a, to, s)
            if d < 3:
                pass_to(a, block(a, to, s), to - way, s, at(way))
            elif d == 3 and (way > 0) == (s == 0):
                pass_to(a, block(a, to, s), 4, s, at(way))
            share(a, block(a, to, s), to, s)

    def partial_sums(k):
        rows = pl.ds(k * chunk, chunk)
        arrived(xg.at[rows, :], "share", k)
        if k == 0:
            for load in mine_in + loads:
                load.wait()
        for i, (values, weight) in enumerate(((xg, wg), (xg, wu), (cg, wd))):
            sums = dot(values[rows, :], weight[...]).astype(BF16)
            part[k, :, :, i * units : (i + 1) * units] = sums.reshape(8, tokens, units)
        for j in (4, 5, 2, 6, 3, 7, 1):
            send(part.at[k, tensor_index(j)], got.at[k, j], (dp, tensor_index(j)), ("sums", k), "sums")

    for d in (1, 2, 3, 4):
        for s in (0, 2):
            for a in (0, 1):
                pass_on(a, d, s)
        if d == 1:
            for a in (0, 1):
                here_now(a, 0, 2)
                share(a, block(a, 0, 2), 0, 2)
        partial_sums(d - 1)

    def finish_units(k):
        arrived(got.at[k, pl.ds(1, 7)], "sums", k)
        total = part[k, me].astype(F32)
        for j in range(1, 8):
            total = total + got[k, j].astype(F32)
        gate, up, grad = (total[:, i * units : (i + 1) * units] for i in range(3))
        sigma = jax.nn.sigmoid(gate)
        silu = gate * sigma
        slope = sigma * (1.0 + gate * (1.0 - sigma))
        mine_now = hh.at[k, me // 2, me % 2]
        mine_now[:, 0:units] = (silu * up).astype(BF16)
        mine_now[:, units : 2 * units] = (grad * up * slope).astype(BF16)
        mine_now[:, 2 * units :] = (grad * silu).astype(BF16)
        for j in (4, 5, 2, 6, 3, 7, 1):
            send(mine_now, mine_now, (dp, tensor_index(j)), ("spread", k), "spread")

    def output_terms(k):
        arrived(got.at[k, pl.ds(1, 7)], "spread", k)
        send(hh.at[k, :, 0], hs.at[k, :, 1], sibling, ("lent",), "lent")
        send(hh.at[k, :, 1], hs.at[k, :, 0], sibling, ("lent",), "lent")
        values = hh[k].reshape(chunk, 3 * units)
        for half in (0, 1):
            if half == 0:
                term = dot_cols(values[:, 0:units], wd[...])
            else:
                term = dot_cols(values[:, units : 2 * units], wg[...])
                term = term + dot_cols(values[:, 2 * units :], wu[...])
            term = term.reshape(2, 2, 2, tokens, width)
            mine[k, half] = term[:, :, 0]
            sib_out[k, half] = term[:, :, 1].astype(BF16)
            send(sib_out.at[k, half], sib_in.at[k, half], sibling, ("handed", k, half), "handed")

    def reduced(d, half):
        k, i = ORDER.index(d) // 2, ORDER.index(d) % 2
        return mine[k, half, i] + sib_in[k, half, i].astype(F32)

    def step(d, half):
        value = reduced(d, half)
        way = 1 if d > 0 else -1
        out = sums_out.at[half, ORDER.index(d)]
        if abs(d) == 2:
            side = 0 if way > 0 else 1
            arrived(met_in.at[half, side], "met", half, side)
            value = value + met_in[half, side, 0:2].astype(F32)
            far = met_in[half, side, 2].astype(F32)
            out[side] = (value[side] + far).astype(BF16)
            out[1 - side] = value[1 - side].astype(BF16)
        else:
            out[...] = value.astype(BF16)
        if d == 4:
            send(out.at[0], met_in.at[half, 0, 2], at(2), ("met", half, 0), "output")
            send(out.at[1], met_in.at[half, 1, 2], at(-2), ("met", half, 1), "output")
        elif abs(d) == 3:
            side = 0 if way > 0 else 1
            send(out, met_in.at[half, side, pl.ds(0, 2)], at(way), ("met", half, side), "output")
        else:
            for s in (0, 1):
                place = ENDS.index((d, s)) if d or s else None
                if place is not None:
                    send(out.at[s], fin.at[half, place], at(d, s), ("ended", half), "output")

    finish_units(2)
    finish_units(3)
    finish_units(1)
    finish_units(0)

    def ready(k, half, steps):
        arrived(sib_in.at[k, half], "handed", k, half)
        for d in steps:
            step(d, half)

    output_terms(2)
    output_terms(3)
    for half in (0, 1):
        ready(2, half, (3,))
    for half in (0, 1):
        ready(3, half, (4, -3))
    output_terms(1)
    for half in (0, 1):
        step(-2, half)
        ready(1, half, (-1, 2))
    output_terms(0)
    for half in (0, 1):
        ready(0, half, (1, 0))

    arrived(hs, "lent")
    rows_all = CHUNKS * chunk
    half_width = width // 2
    tile = 128
    here = pl.multiple_of(core * units, units)
    there = pl.multiple_of((1 - core) * units, units)
    stores = []
    for m, values in enumerate((cg, xg, xg)):

        def weight_tile(i, carry):
            at_col = pl.multiple_of(core * half_width + i * tile, tile)
            at_row = pl.multiple_of(i * tile, tile)
            left = values[:, pl.ds(at_col, tile)]
            for source, place in ((hh, here), (hs, there)):
                right = source[:, :, :, :, m * units : (m + 1) * units].reshape(rows_all, units)
                gw[m, pl.ds(at_row, tile), pl.ds(place, units)] = dot_rows(left, right).astype(BF16)
            return carry

        lax.fori_loop(0, half_width // tile, weight_tile, 0)
        stores.append(pltpu.make_async_copy(gw.at[m], gw_out.at[m], osem.at[m]))
        stores[m].start()

    for half, out_ref in enumerate((lo_ref, tg_ref)):
        arrived(fin.at[half], "ended", half)
        total = mine[0, half, 0, 0] + sib_in[0, half, 0, 0].astype(F32)
        for place in range(len(ENDS)):
            total = total + fin[half, place].astype(F32)
        out_ref[...] = total.astype(BF16)
    for a in (0, 1):
        left(xg.at[pl.ds(0, 31 * tokens), :], f"gather{a}")
    left(got.at[:, pl.ds(1, 7)], "sums")
    left(got.at[:, pl.ds(1, 7)], "spread")
    left(hs, "lent")
    left(sib_in, "handed")
    left(xg.at[pl.ds(0, 30 * tokens), :], "output")
    for store in stores:
        store.wait()


def store_results(lo, tg, gw, lo_out, tg_out, gate_out, up_out, down_out, stage, in_sem, out_sem):
    rows = gw.shape[1] // 2
    loads, copies = [], []
    for m, out in enumerate((down_out, gate_out, up_out)):
        for i in range(2):
            part = pl.ds(i * rows, rows)
            n = 2 * m + i
            loads.append(pltpu.make_async_copy(gw.at[m, part], stage.at[m, part], in_sem.at[n]))
            copies.append(pltpu.make_async_copy(stage.at[m, part], out.at[part], out_sem.at[n]))
    ends = [
        pltpu.make_async_copy(src, dst, out_sem.at[6 + i])
        for i, (src, dst) in enumerate(((lo, lo_out), (tg, tg_out)))
    ]
    for copy in loads + ends:
        copy.start()
    for load, copy in zip(loads, copies):
        load.wait()
        copy.start()
    for copy in copies + ends:
        copy.wait()


def shards(layer_input, out_cotangent, old_gate, old_up, old_down):
    tokens, width = layer_input.shape
    units = old_gate.shape[1]
    all_tokens = 32 * tokens
    vmem = pl.BlockSpec(memory_space=pltpu.VMEM)
    hbm = pl.BlockSpec(memory_space=pltpu.HBM)
    grad_shape = jax.ShapeDtypeStruct((width // 2, 2 * units), BF16)
    out_shape = jax.ShapeDtypeStruct((tokens, width), BF16)
    results = pl.pallas_call(
        kernel,
        out_shape=(out_shape, out_shape, jax.ShapeDtypeStruct((3,) + grad_shape.shape, BF16)),
        in_specs=[hbm] * 5,
        out_specs=[vmem, vmem, hbm],
        scratch_shapes=[
            pltpu.VMEM((width, units), BF16),
            pltpu.VMEM((width, units), BF16),
            pltpu.VMEM((width, units), BF16),
            pltpu.VMEM((all_tokens, width), BF16),
            pltpu.VMEM((all_tokens, width), BF16),
            pltpu.VMEM((CHUNKS, 8, tokens, 3 * units), BF16),
            pltpu.VMEM((CHUNKS, 8, tokens, 3 * units), BF16),
            pltpu.VMEM((CHUNKS, 4, 2, tokens, 3 * units), BF16),
            pltpu.VMEM((CHUNKS, 4, 2, tokens, 3 * units), BF16),
            pltpu.VMEM((CHUNKS, 2, 2, 2, tokens, width), F32),
            pltpu.VMEM((CHUNKS, 2, 2, 2, tokens, width), BF16),
            pltpu.VMEM((CHUNKS, 2, 2, 2, tokens, width), BF16),
            pltpu.VMEM((2, 8, 2, tokens, width), BF16),
            pltpu.VMEM((2, 2, 3, tokens, width), BF16),
            pltpu.VMEM((2, len(ENDS), tokens, width), BF16),
            pltpu.VMEM((3, width // 2, 2 * units), BF16),
            pltpu.SemaphoreType.DMA((5,)),
            pltpu.SemaphoreType.DMA((3,)),
            pltpu.SemaphoreType.DMA((SENDS,)),
            pltpu.SemaphoreType.DMA((RECEIVES,)),
        ],
        compiler_params=pltpu.CompilerParams(
            collective_id=0, has_side_effects=True, vmem_limit_bytes=63 * 1024 * 1024
        ),
        cost_estimate=pl.CostEstimate(
            flops=18 * all_tokens * width * units, bytes_accessed=12 * width * units, transcendentals=0
        ),
    )(layer_input, out_cotangent, old_gate, old_up, old_down)
    return pl.pallas_call(
        store_results,
        out_shape=(out_shape, out_shape, grad_shape, grad_shape, grad_shape),
        in_specs=[vmem, vmem, hbm],
        out_specs=[hbm] * 5,
        scratch_shapes=[
            pltpu.VMEM((3,) + grad_shape.shape, BF16),
            pltpu.SemaphoreType.DMA((6,)),
            pltpu.SemaphoreType.DMA((8,)),
        ],
        compiler_params=pltpu.CompilerParams(vmem_limit_bytes=63 * 1024 * 1024),
    )(*results)


def solution(mesh):
    wide = P("dp", "tensor")
    stored = P("tensor", "dp")
    return jax.shard_map(
        shards,
        mesh=mesh,
        in_specs=(wide, wide, stored, stored, stored),
        out_specs=(wide, wide, stored, stored, stored),
        check_vma=False,
    )
```

time: 82.7 us -> 73.9 us (0.89)
  the two profiles are of different devices: /device:TPU:32 before, /device:TPU:1 now
where the time goes in v2:
time: 73.9 us; the launch traced here: 73.7 us
  Pallas kernels  73.1 us (99%)
    pallas_call x1, Pallas kernels, shards(): pl.pallas_call(kernel, out_shape=(out_shape, out_shape, jax.ShapeDtypeStr...  69.5 us
    pallas_call x1, Pallas kernels, shards(): pl.pallas_call(store_results, out_shape=(out_shape, out_shape, grad_shape...  3.62 us

profile of v2, /device:TPU:1, one launch (start us, length us, event | category | flops | bytes accessed | tf_op | source)
XLA Modules:
  0.0 73.7 jit_solution(13309693774183010535)
XLA Ops:
  0.6 69.5 %shard_map.92 = (bf16[16,1024]{1,0:T(8,128)(2,1)}, bf16[16,1024]{1,0:T(8,128)(2,1)}, bf16[3,512,1024]{2,1,0:T(8,128)(2,1)}) custom-call(bf16[16,1024]{1,0:T(8,128)(2,1)} %x_ref.1, bf16[16,1024]{1,0:T(8,128)(2,1)} %c_ref.1, bf16[1024,512]{1,0:T(8,128)(2,1)} %wg_any.1, bf16[1024,512]{1,0:T(8,128)(2,1)} %wu_any.1, bf16[1024,512]{1,0:T(8,128)(2,1)} %wd_any.1), custom_call_target="tpu_custom_call" | custom-call | flops 4831838208 | bytes 6291456 | tf_op jit(solution)/shard_map/pallas_call | solution.py:306
  70.1 3.6 %shard_map.93 = (bf16[16,1024]{1,0:T(8,128)(2,1)}, bf16[16,1024]{1,0:T(8,128)(2,1)}, bf16[512,1024]{1,0:T(8,128)(2,1)}, bf16[512,1024]{1,0:T(8,128)(2,1)}, bf16[512,1024]{1,0:T(8,128)(2,1)}) custom-call(bf16[16,1024]{1,0:T(8,128)(2,1)} %get-tuple-element.8.lo, bf16[16,1024]{1,0:T(8,128)(2,1)} %get-tuple-element.9.tg, bf16[3,512,1024]{2,1,0:T(8,128)(2,1)} %get-tuple-element.10.gw), custom_call_target="tpu_custom_call" | custom-call | tf_op jit(solution)/shard_map/pallas_call | solution.py:340

commit v3 on v2

v3 whole, which is shorter than its diff:
```python
import jax
import jax.numpy as jnp
from jax import lax
from jax.experimental import pallas as pl
from jax.experimental.pallas import tpu as pltpu
from jax.sharding import PartitionSpec as P

MESH = pl.DeviceIdType.MESH
F32 = jnp.float32
BF16 = jnp.bfloat16

ENTRIES = (
    (0, 0), (0, 1), (1, 0), (-1, 0),
    (1, 1), (-1, 1), (2, 0), (-2, 0),
    (2, 1), (-2, 1), (3, 1), (-3, 0),
    (3, 0), (-3, 1), (4, 0), (4, 1),
)
CHUNKS = 4
DIRECT = (1, 2, 3)
SENDS, RECEIVES = 12, 30 + 8 + 4 * (CHUNKS - len(DIRECT)) + len(DIRECT) + 23
CUT = 640
FIRST, SECOND = pl.ds(0, CUT), pl.ds(CUT, 1536 - CUT)
ENDS = ((2, 0), (-2, 1), (1, 0), (1, 1), (-1, 0), (-1, 1), (0, 1))


def dot(a, b):
    return jnp.dot(a, b, preferred_element_type=F32)


def dot_cols(a, b):
    return lax.dot_general(a, b, (((1,), (1,)), ((), ())), preferred_element_type=F32)


def dot_rows(a, b):
    return lax.dot_general(a, b, (((0,), (0,)), ((), ())), preferred_element_type=F32)


def kernel(
    x_ref, c_ref, wg_any, wu_any, wd_any,
    lo_ref, tg_ref, gw_out,
    wg, wu, wd, xg, cg, part, in_x, in_y, out_x, out_y, end_x, end_y, kept, got, hh, hs, mine, sib_out, sib_in, sums_out, met_in, fin, gw,
    wsem, osem, ssem, rsem,
):
    dp = lax.axis_index("dp")
    me = lax.axis_index("tensor")
    core, yh, z = dp % 2, (dp // 2) % 2, dp // 4
    x, yl = me // 2, me % 2
    tokens, width = x_ref.shape
    units = wg_any.shape[1]
    chunk = 8 * tokens

    def at(dz, flip_y=0, flip_core=0):
        return (((z + dz + 8) % 8) * 4 + ((yh + flip_y) % 2) * 2 + (core + flip_core) % 2, me)

    def x_of(j):
        return (x, x + 1 - 2 * (x % 2), (x + 2) % 4, 3 - x)[j]

    def peer_of(j):
        return (dp, x_of(j // 2) * 2 + (yl + j % 2) % 2)

    def x_peer(j):
        return peer_of(2 * j)

    y_peer = peer_of(1)
    sibling = at(0, 0, 1)
    loads = [
        pltpu.make_async_copy(src, dst, wsem.at[i])
        for i, (src, dst) in enumerate(((wg_any, wg), (wu_any, wu), (wd_any, wd)))
    ]
    mine_in = [
        pltpu.make_async_copy(src, dst.at[pl.ds(0, tokens), :], wsem.at[3 + i])
        for i, (src, dst) in enumerate(((x_ref, xg), (c_ref, cg)))
    ]
    for load in mine_in + loads:
        load.start()

    barrier = pltpu.get_barrier_semaphore()
    peers = [at(1), at(-1), at(1, 1), at(-1, 1), at(0, 1), sibling]
    peers += [at(2), at(-2), at(2, 1), at(-2, 1)]
    peers += [peer_of(j) for j in range(1, 8)]
    for peer in peers:
        pl.semaphore_signal(barrier, inc=1, device_id=peer, device_id_type=MESH)
    pl.semaphore_wait(barrier, len(peers))

    places = {}

    def place_of(kind, key):
        return places.setdefault((kind, key), sum(1 for k, _ in places if k == kind))

    def send(src, dst, device, key, group):
        copy = pltpu.make_async_remote_copy(
            src_ref=src, dst_ref=dst, send_sem=ssem.at[place_of("send", group)], recv_sem=rsem.at[place_of("recv", key)],
            device_id=device, device_id_type=MESH,
        )
        copy.start()

    def of_size(ref, key, group):
        return pltpu.make_async_remote_copy(
            src_ref=ref, dst_ref=ref, send_sem=ssem.at[place_of("send", group)], recv_sem=rsem.at[place_of("recv", key)],
            device_id=sibling, device_id_type=MESH,
        )

    def arrived(ref, *key):
        of_size(ref, key, "gather0").wait_recv()

    def left(ref, group):
        of_size(ref, ("gather", 0, 1, 0), group).wait_send()

    held = (xg, cg)
    own = (x_ref, c_ref)

    def block(a, d, s):
        return held[a].at[pl.ds((ENTRIES.index((d, s // 2)) * 2 + s % 2) * tokens, tokens), :]

    def pass_to(a, src, d, s, device):
        send(src, block(a, d, s), device, ("gather", a, d, s), f"gather{a}")

    def share(a, src, d, s):
        send(src, block(a, d, s + 1), sibling, ("share", ENTRIES.index((d, s // 2)) // 4), f"gather{a}")

    def here_now(a, d, s):
        arrived(block(a, d, s), "gather", a, d, s)

    for a in (0, 1):
        pass_to(a, own[a], -1, 0, at(1))
        pass_to(a, own[a], 1, 0, at(-1))
        pass_to(a, own[a], -1, 2, at(1, 1))
        pass_to(a, own[a], 1, 2, at(-1, 1))
        pass_to(a, own[a], 0, 2, at(0, 1))
        share(a, own[a], 0, 0)

    def pass_on(a, d, s):
        for way in (1, -1):
            to = -way * d if d < 4 else 4
            if d == 4 and (way > 0) != (s == 0):
                continue
            here_now(a, to, s)
            if d < 3:
                pass_to(a, block(a, to, s), to - way, s, at(way))
            elif d == 3 and (way > 0) == (s == 0):
                pass_to(a, block(a, to, s), 4, s, at(way))
            share(a, block(a, to, s), to, s)

    def own_pair(a):
        here_now(a, 0, 2)
        share(a, block(a, 0, 2), 0, 2)

    def partial_sums(k):
        rows = pl.ds(k * chunk, chunk)
        arrived(xg.at[rows, :], "share", k)
        if k == 0:
            for load in mine_in + loads:
                load.wait()
        for i, (values, weight) in enumerate(((xg, wg), (xg, wu), (cg, wd))):
            sums = dot(values[rows, :], weight[...]).astype(BF16)
            part[k, :, :, :, i * units : (i + 1) * units] = sums.reshape(4, 2, tokens, units)
        if k in DIRECT:
            for j in (4, 5, 2, 6, 3, 7, 1):
                src = part.at[k, x_of(j // 2), (yl + j % 2) % 2]
                send(src, got.at[DIRECT.index(k), j - 1], peer_of(j), ("sums", k), "sums")
            return
        send(part.at[k, :, 1 - yl, :, SECOND], in_y.at[k], y_peer, ("sums y", k), "sums y")
        for j in (2, 1, 3):
            send(part.at[k, x_of(j), :, :, FIRST], in_x.at[k, j - 1], x_peer(j), ("sums x", k), "sums x")

    def mix_sums(k):
        arrived(in_y.at[k], "sums y", k)
        both = part[k, :, yl, :, SECOND].astype(F32) + in_y[k].astype(F32)
        out_y[k] = both.astype(BF16)
        for j in (2, 1, 3):
            send(out_y.at[k, x_of(j)], end_x.at[k, j - 1], x_peer(j), ("mixed x", k), "mixed x")
        arrived(in_x.at[k], "sums x", k)
        theirs, ours = part[k, x, 1 - yl, :, FIRST].astype(F32), part[k, x, yl, :, FIRST].astype(F32)
        for j in range(3):
            theirs = theirs + in_x[k, j, 1 - yl].astype(F32)
            ours = ours + in_x[k, j, yl].astype(F32)
        out_x[k] = theirs.astype(BF16)
        kept[k] = ours
        send(out_x.at[k], end_y.at[k], y_peer, ("mixed y", k), "mixed y")

    def finish_units(k):
        if k in DIRECT:
            mail = got.at[DIRECT.index(k)]
            arrived(mail, "sums", k)
            total = part[k, x, yl].astype(F32)
            for j in range(7):
                total = total + mail[j].astype(F32)
        else:
            arrived(end_x.at[k], "mixed x", k)
            arrived(end_y.at[k], "mixed y", k)
            first = kept[k] + end_y[k].astype(F32)
            second = out_y[k, x].astype(F32)
            for j in range(3):
                second = second + end_x[k, j].astype(F32)
            total = jnp.concatenate([first, second], axis=1)
        gate, up, grad = (total[:, i * units : (i + 1) * units] for i in range(3))
        sigma = jax.nn.sigmoid(gate)
        silu = gate * sigma
        slope = sigma * (1.0 + gate * (1.0 - sigma))
        mine_now = hh.at[k, x, yl]
        mine_now[:, 0:units] = (silu * up).astype(BF16)
        mine_now[:, units : 2 * units] = (grad * up * slope).astype(BF16)
        mine_now[:, 2 * units :] = (grad * silu).astype(BF16)
        for j in (4, 5, 2, 6, 3, 7, 1):
            send(mine_now, mine_now, peer_of(j), ("spread", k), "spread last" if j == 1 else "spread")

    def output_terms(k):
        arrived(got.at[0], "spread", k)
        send(hh.at[k, :, 0], hs.at[k, :, 1], sibling, ("lent",), "lent")
        send(hh.at[k, :, 1], hs.at[k, :, 0], sibling, ("lent",), "lent")
        values = hh[k].reshape(chunk, 3 * units)
        for half in (0, 1):
            if half == 0:
                term = dot_cols(values[:, 0:units], wd[...])
            else:
                term = dot_cols(values[:, units : 2 * units], wg[...])
                term = term + dot_cols(values[:, 2 * units :], wu[...])
            term = term.reshape(4, 2, tokens, width)
            mine[k, half] = term[:, 0]
            sib_out[k, half] = term[:, 1].astype(BF16)
            send(sib_out.at[k, half], sib_in.at[k, half], sibling, ("handed", k, half), "handed")

    def step(d, h, half):
        entry = ENTRIES.index((d, h))
        value = mine[entry // 4, half, entry % 4] + sib_in[entry // 4, half, entry % 4].astype(F32)
        side = 0 if d > 0 else 1
        out = sums_out.at[half, entry]
        if abs(d) == 2 and h == side:
            arrived(met_in.at[half, side, pl.ds(0, 2)], "met", half, side, h)
            value = value + met_in[half, side, 0].astype(F32) + met_in[half, side, 1].astype(F32)
        elif abs(d) == 2:
            arrived(met_in.at[half, side, 2], "met", half, side, h)
            value = value + met_in[half, side, 2].astype(F32)
        elif abs(d) == 1 and h != side:
            arrived(met_in.at[half, side, 3], "near", half, side)
            value = value + met_in[half, side, 3].astype(F32)
        out[...] = value.astype(BF16)
        if d == 4:
            send(out, met_in.at[half, h, 1], at(2 if h == 0 else -2), ("met", half, h, h), "output")
        elif abs(d) == 3:
            send(out, met_in.at[half, side, 0 if h == side else 2], at(1 if d > 0 else -1), ("met", half, side, h), "output")
        elif abs(d) == 2 and h != side:
            send(out, met_in.at[half, side, 3], at(1 if d > 0 else -1), ("near", half, side), "output")
        else:
            send(out, fin.at[half, ENDS.index((d, h))], at(d, h), ("ended", half), "output")

    def steps(k, *which):
        for half in (0, 1):
            if k is not None:
                arrived(sib_in.at[k, half], "handed", k, half)
            for d, h in which:
                step(d, h, half)

    X, C = 0, 1
    pass_on(X, 1, 0)
    own_pair(X)
    pass_on(C, 1, 0)
    own_pair(C)
    pass_on(X, 1, 2)
    pass_on(X, 2, 0)
    partial_sums(0)
    pass_on(C, 1, 2)
    pass_on(C, 2, 0)
    pass_on(X, 2, 2)
    pass_on(X, 3, 0)
    pass_on(C, 2, 2)
    partial_sums(1)
    pass_on(C, 3, 0)
    pass_on(X, 3, 2)
    pass_on(X, 4, 0)
    pass_on(C, 3, 2)
    mix_sums(0)
    pass_on(C, 4, 0)
    pass_on(X, 4, 2)
    partial_sums(2)
    pass_on(C, 4, 2)
    partial_sums(3)
    finish_units(2)
    finish_units(3)
    finish_units(1)
    finish_units(0)
    output_terms(2)
    output_terms(3)
    steps(2, (3, 1), (-3, 0))
    steps(3, (4, 0), (4, 1), (3, 0), (-3, 1))
    output_terms(1)
    steps(None, (2, 1))
    steps(1, (-1, 1), (-2, 0))
    output_terms(0)
    steps(None, (1, 1))
    steps(0, (0, 1), (1, 0))
    steps(None, (2, 0), (-2, 1))
    steps(None, (-1, 0))

    arrived(hs, "lent")
    rows_all = CHUNKS * chunk
    half_width = width // 2
    tile = 256
    here = pl.multiple_of(core * units, units)
    there = pl.multiple_of((1 - core) * units, units)
    stores = []
    for m, values in enumerate((cg, xg, xg)):

        def weight_tile(i, carry):
            at_col = pl.multiple_of(core * half_width + i * tile, tile)
            at_row = pl.multiple_of(i * tile, tile)
            left = values[:, pl.ds(at_col, tile)]
            for source, place in ((hh, here), (hs, there)):
                right = source[:, :, :, :, m * units : (m + 1) * units].reshape(rows_all, units)
                gw[m, pl.ds(at_row, tile), pl.ds(place, units)] = dot_rows(left, right).astype(BF16)
            return carry

        lax.fori_loop(0, half_width // tile, weight_tile, 0)
        stores.append(pltpu.make_async_copy(gw.at[m], gw_out.at[m], osem.at[m]))
        stores[m].start()

    for half, out_ref in enumerate((lo_ref, tg_ref)):
        arrived(fin.at[half], "ended", half)
        total = mine[0, half, 0] + sib_in[0, half, 0].astype(F32)
        for place in range(len(ENDS)):
            total = total + fin[half, place].astype(F32)
        out_ref[...] = total.astype(BF16)
    for a in (0, 1):
        left(xg.at[pl.ds(0, 31 * tokens), :], f"gather{a}")
    two = pl.ds(0, CHUNKS - len(DIRECT))
    left(in_y.at[two], "sums y")
    left(in_x.at[two], "sums x")
    left(end_x.at[two], "mixed x")
    left(end_y.at[two], "mixed y")
    left(got, "sums")
    left(hh.at[:, pl.ds(0, 3), :], "spread")
    left(hh.at[:, 0, 0], "spread last")
    left(hs, "lent")
    left(sib_in, "handed")
    left(xg.at[pl.ds(0, 30 * tokens), :], "output")
    for store in stores:
        store.wait()
    kinds = [kind for kind, _ in places]
    assert (kinds.count("send"), kinds.count("recv")) == (SENDS, RECEIVES)


def store_results(lo, tg, gw, lo_out, tg_out, gate_out, up_out, down_out, stage, small, in_sem, out_sem):
    rows = gw.shape[1] // 2
    moves = []
    for m, out in enumerate((down_out, gate_out, up_out)):
        for i in range(2):
            part = pl.ds(i * rows, rows)
            moves.append((gw.at[m, part], stage.at[m, part], out.at[part]))
    moves += [(lo, small.at[0], lo_out), (tg, small.at[1], tg_out)]
    loads = [pltpu.make_async_copy(src, via, in_sem.at[n]) for n, (src, via, _) in enumerate(moves)]
    stores = [pltpu.make_async_copy(via, dst, out_sem.at[n]) for n, (_, via, dst) in enumerate(moves)]
    for load in loads:
        load.start()
    for load, store in zip(loads, stores):
        load.wait()
        store.start()
    for store in stores:
        store.wait()


def shards(layer_input, out_cotangent, old_gate, old_up, old_down):
    tokens, width = layer_input.shape
    units = old_gate.shape[1]
    all_tokens = 32 * tokens
    vmem = pl.BlockSpec(memory_space=pltpu.VMEM)
    hbm = pl.BlockSpec(memory_space=pltpu.HBM)
    grad_shape = jax.ShapeDtypeStruct((width // 2, 2 * units), BF16)
    out_shape = jax.ShapeDtypeStruct((tokens, width), BF16)
    results = pl.pallas_call(
        kernel,
        out_shape=(out_shape, out_shape, jax.ShapeDtypeStruct((3,) + grad_shape.shape, BF16)),
        in_specs=[hbm] * 5,
        out_specs=[vmem, vmem, hbm],
        scratch_shapes=[
            pltpu.VMEM((width, units), BF16),
            pltpu.VMEM((width, units), BF16),
            pltpu.VMEM((width, units), BF16),
            pltpu.VMEM((all_tokens, width), BF16),
            pltpu.VMEM((all_tokens, width), BF16),
            pltpu.VMEM((CHUNKS, 4, 2, tokens, 3 * units), BF16),
            pltpu.VMEM((CHUNKS, 3, 2, tokens, CUT), BF16),
            pltpu.VMEM((CHUNKS, 4, tokens, 3 * units - CUT), BF16),
            pltpu.VMEM((CHUNKS, tokens, CUT), BF16),
            pltpu.VMEM((CHUNKS, 4, tokens, 3 * units - CUT), BF16),
            pltpu.VMEM((CHUNKS, 3, tokens, 3 * units - CUT), BF16),
            pltpu.VMEM((CHUNKS, tokens, CUT), BF16),
            pltpu.VMEM((CHUNKS, tokens, CUT), F32),
            pltpu.VMEM((len(DIRECT), 7, tokens, 3 * units), BF16),
            pltpu.VMEM((CHUNKS, 4, 2, tokens, 3 * units), BF16),
            pltpu.VMEM((CHUNKS, 4, 2, tokens, 3 * units), BF16),
            pltpu.VMEM((CHUNKS, 2, 4, tokens, width), F32),
            pltpu.VMEM((CHUNKS, 2, 4, tokens, width), BF16),
            pltpu.VMEM((CHUNKS, 2, 4, tokens, width), BF16),
            pltpu.VMEM((2, 16, tokens, width), BF16),
            pltpu.VMEM((2, 2, 4, tokens, width), BF16),
            pltpu.VMEM((2, len(ENDS), tokens, width), BF16),
            pltpu.VMEM((3, width // 2, 2 * units), BF16),
            pltpu.SemaphoreType.DMA((5,)),
            pltpu.SemaphoreType.DMA((3,)),
            pltpu.SemaphoreType.DMA((SENDS,)),
            pltpu.SemaphoreType.DMA((RECEIVES,)),
        ],
        compiler_params=pltpu.CompilerParams(
            collective_id=0, has_side_effects=True, vmem_limit_bytes=63 * 1024 * 1024
        ),
        cost_estimate=pl.CostEstimate(
            flops=18 * all_tokens * width * units, bytes_accessed=12 * width * units, transcendentals=0
        ),
    )(layer_input, out_cotangent, old_gate, old_up, old_down)
    return pl.pallas_call(
        store_results,
        out_shape=(out_shape, out_shape, grad_shape, grad_shape, grad_shape),
        in_specs=[hbm] * 3,
        out_specs=[hbm] * 5,
        scratch_shapes=[
            pltpu.VMEM((3,) + grad_shape.shape, BF16),
            pltpu.VMEM((2,) + out_shape.shape, BF16),
            pltpu.SemaphoreType.DMA((8,)),
            pltpu.SemaphoreType.DMA((8,)),
        ],
        compiler_params=pltpu.CompilerParams(vmem_limit_bytes=63 * 1024 * 1024),
    )(*results)


def solution(mesh):
    wide = P("dp", "tensor")
    stored = P("tensor", "dp")
    return jax.shard_map(
        shards,
        mesh=mesh,
        in_specs=(wide, wide, stored, stored, stored),
        out_specs=(wide, wide, stored, stored, stored),
        check_vma=False,
    )
```

time: 73.9 us -> 70.8 us (0.958)
  Pallas kernels: 73.1 us -> 70.1 us
    pallas_call x1, Pallas kernels: 69.5 us -> 67.2 us  [shards(): pl.pallas_call(kernel, out_shape=(out_shape, out_shape, jax.ShapeDtypeStr...]
    pallas_call x1, Pallas kernels: 3.62 us -> 2.84 us  [shards(): pl.pallas_call(store_results, out_shape=(out_shape, out_shape, grad_shape...]
where the time goes in v3:
time: 70.8 us; the launch traced here: 70.7 us
  Pallas kernels  70.1 us (99%)
    pallas_call x1, Pallas kernels, shards(): pl.pallas_call(kernel, out_shape=(out_shape, out_shape, jax.ShapeDtypeStr...  67.2 us
    pallas_call x1, Pallas kernels, shards(): pl.pallas_call(store_results, out_shape=(out_shape, out_shape, grad_shape...  2.84 us

profile of v3, /device:TPU:1, one launch (start us, length us, event | category | flops | bytes accessed | tf_op | source)
XLA Modules:
  0.0 70.7 jit_solution(4785148014239337413)
XLA Ops:
  0.6 67.2 %shard_map.92 = (bf16[16,1024]{1,0:T(8,128)(2,1)}, bf16[16,1024]{1,0:T(8,128)(2,1)}, bf16[3,512,1024]{2,1,0:T(8,128)(2,1)}) custom-call(bf16[16,1024]{1,0:T(8,128)(2,1)} %x_ref.1, bf16[16,1024]{1,0:T(8,128)(2,1)} %c_ref.1, bf16[1024,512]{1,0:T(8,128)(2,1)} %wg_any.1, bf16[1024,512]{1,0:T(8,128)(2,1)} %wu_any.1, bf16[1024,512]{1,0:T(8,128)(2,1)} %wd_any.1), custom_call_target="tpu_custom_call" | custom-call | flops 4831838208 | bytes 6291456 | tf_op jit(solution)/shard_map/pallas_call | solution.py:369
  67.9 2.8 %shard_map.93 = (bf16[16,1024]{1,0:T(8,128)(2,1)}, bf16[16,1024]{1,0:T(8,128)(2,1)}, bf16[512,1024]{1,0:T(8,128)(2,1)}, bf16[512,1024]{1,0:T(8,128)(2,1)}, bf16[512,1024]{1,0:T(8,128)(2,1)}) custom-call(bf16[16,1024]{1,0:T(8,128)(2,1)} %get-tuple-element.8.lo, bf16[16,1024]{1,0:T(8,128)(2,1)} %get-tuple-element.9.tg, bf16[3,512,1024]{2,1,0:T(8,128)(2,1)} %get-tuple-element.10.gw), custom_call_target="tpu_custom_call" | custom-call | tf_op jit(solution)/shard_map/pallas_call | solution.py:410

commit v4 on v3

--- a/solution.py
+++ b/solution.py
@@ -155,7 +155,7 @@
             sums = dot(values[rows, :], weight[...]).astype(BF16)
             part[k, :, :, :, i * units : (i + 1) * units] = sums.reshape(4, 2, tokens, units)
         if k in DIRECT:
-            for j in (4, 5, 2, 6, 3, 7, 1):
+            for j in (5, 4, 7, 3, 6, 2, 1):
                 src = part.at[k, x_of(j // 2), (yl + j % 2) % 2]
                 send(src, got.at[DIRECT.index(k), j - 1], peer_of(j), ("sums", k), "sums")
             return
@@ -201,7 +201,7 @@
         mine_now[:, 0:units] = (silu * up).astype(BF16)
         mine_now[:, units : 2 * units] = (grad * up * slope).astype(BF16)
         mine_now[:, 2 * units :] = (grad * silu).astype(BF16)
-        for j in (4, 5, 2, 6, 3, 7, 1):
+        for j in (5, 4, 7, 3, 6, 2, 1):
             send(mine_now, mine_now, peer_of(j), ("spread", k), "spread last" if j == 1 else "spread")
 
     def output_terms(k):
@@ -262,9 +262,9 @@
     pass_on(C, 1, 2)
     pass_on(C, 2, 0)
     pass_on(X, 2, 2)
+    partial_sums(1)
     pass_on(X, 3, 0)
     pass_on(C, 2, 2)
-    partial_sums(1)
     pass_on(C, 3, 0)
     pass_on(X, 3, 2)
     pass_on(X, 4, 0)
@@ -282,10 +282,10 @@
     output_terms(2)
     output_terms(3)
     steps(2, (3, 1), (-3, 0))
-    steps(3, (4, 0), (4, 1), (3, 0), (-3, 1))
+    steps(3, (3, 0), (-3, 1), (4, 0), (4, 1))
     output_terms(1)
     steps(None, (2, 1))
-    steps(1, (-1, 1), (-2, 0))
+    steps(1, (-2, 0), (-1, 1))
     output_terms(0)
     steps(None, (1, 1))
     steps(0, (0, 1), (1, 0))

time: 70.8 us -> 69.5 us (0.982)
  Pallas kernels: 70.1 us -> 68.7 us
    pallas_call x1, Pallas kernels: 67.2 us -> 65.9 us  [shards(): pl.pallas_call(kernel, out_shape=(out_shape, out_shape, jax.ShapeDtypeStr...]
where the time goes in v4:
time: 69.5 us; the launch traced here: 69.4 us
  Pallas kernels  68.7 us (99%)
    pallas_call x1, Pallas kernels, shards(): pl.pallas_call(kernel, out_shape=(out_shape, out_shape, jax.ShapeDtypeStr...  65.9 us
    pallas_call x1, Pallas kernels, shards(): pl.pallas_call(store_results, out_shape=(out_shape, out_shape, grad_shape...  2.84 us

profile of v4, /device:TPU:1, one launch (start us, length us, event | category | flops | bytes accessed | tf_op | source)
XLA Modules:
  0.0 69.4 jit_solution(290015914227786388)
XLA Ops:
  0.6 65.9 %shard_map.92 = (bf16[16,1024]{1,0:T(8,128)(2,1)}, bf16[16,1024]{1,0:T(8,128)(2,1)}, bf16[3,512,1024]{2,1,0:T(8,128)(2,1)}) custom-call(bf16[16,1024]{1,0:T(8,128)(2,1)} %x_ref.1, bf16[16,1024]{1,0:T(8,128)(2,1)} %c_ref.1, bf16[1024,512]{1,0:T(8,128)(2,1)} %wg_any.1, bf16[1024,512]{1,0:T(8,128)(2,1)} %wu_any.1, bf16[1024,512]{1,0:T(8,128)(2,1)} %wd_any.1), custom_call_target="tpu_custom_call" | custom-call | flops 4831838208 | bytes 6291456 | tf_op jit(solution)/shard_map/pallas_call | solution.py:369
  66.5 2.8 %shard_map.93 = (bf16[16,1024]{1,0:T(8,128)(2,1)}, bf16[16,1024]{1,0:T(8,128)(2,1)}, bf16[512,1024]{1,0:T(8,128)(2,1)}, bf16[512,1024]{1,0:T(8,128)(2,1)}, bf16[512,1024]{1,0:T(8,128)(2,1)}) custom-call(bf16[16,1024]{1,0:T(8,128)(2,1)} %get-tuple-element.8.lo, bf16[16,1024]{1,0:T(8,128)(2,1)} %get-tuple-element.9.tg, bf16[3,512,1024]{2,1,0:T(8,128)(2,1)} %get-tuple-element.10.gw), custom_call_target="tpu_custom_call" | custom-call | tf_op jit(solution)/shard_map/pallas_call | solution.py:410
